TPU v7x, 512 devices: a whole 4x4x16 slice. The times are simulated.
512 devices in a mesh: ctx: 16 (over y, z_hi, core), exp: 32 (over x, z_lo).
Axes of the slice: x: 4, y: 4, z: 16 (z_hi: 2, z_lo: 8; z = z_hi * 8 + z_lo), core: 2. Of those that a mesh axis runs over, the one named last changes fastest.
Arguments:
- queries: bfloat16 [16, 32, 64, 4096], P('ctx', 'exp'), may hold values from -90 to 90
- new_keys_values: bfloat16 [16, 32, 64, 512], P('ctx', 'exp'), may hold values from -4.5 to 4.5
- cached_keys_values: bfloat16 [16, 32, 64, 512], P('ctx', 'exp'), may hold values from -4.5 to 4.5
- residual: bfloat16 [16, 32, 64, 4096], P(None, 'exp', None, 'ctx'), may hold values from -17 to 17
- out_weight: bfloat16 [4096, 4096], P('exp', 'ctx'), may hold values from -0.1875 to 0.1875
- norm_gain: float32 [4096], P('ctx'), may hold values from 0.1 to 1.9
- routes: int32 [16, 32, 64, 8], P(None, 'exp'), may hold values from 0 to 127, as said below
- gates: float32 [16, 32, 64, 8], P(None, 'exp'), may hold values from 0.3 to 1
- w_gate_up: bfloat16 [32, 4096, 3072], P('exp', 'ctx'), may hold values from -0.125 to 0.125
- w_down: bfloat16 [32, 1536, 4096], P('exp', None, 'ctx'), may hold values from -0.15625 to 0.15625
Outputs:
- layer_out: bfloat16 [16, 32, 64, 4096], P(None, 'exp', None, 'ctx')
Inputs may be any that keep to these rules, and one draw needn't show every extreme that they name: `routes`: each row names 8 different experts, at most one of them below 32. Among the rows that share the second index, an expert below 32 is named by at most 16 of them, and some expert by exactly 16.
All inputs are finite; a program needn't handle non-finite values.
Results may differ from a plain program's by a relative error of at most 0.02.
Values may be sent and summed in bfloat16 or wider, within the bound.
A program may use at most 64 MiB of HBM per device.

v0:
```python
import jax
import jax.numpy as jnp
from jax import lax
from jax.sharding import PartitionSpec as P

D = 4096
QUERY_HEADS = 32
KEY_VALUE_HEADS = 2
HEAD_SIZE = 128


NEG_FILL = -1e30


def body(
    queries,
    new_keys_values,
    cached_keys_values,
    residual,
    out_weight,
    norm_gain,
    routes,
    gates,
    w_gate_up,
    w_down,
):
    groups = lax.axis_size("ctx")
    experts_here = lax.axis_size("exp")
    tok_dev = queries.shape[2]
    past_dev = cached_keys_values.shape[2]
    tok_rows = groups * tok_dev
    past_rows = groups * past_dev
    width_block = residual.shape[3]
    hidden = w_down.shape[1]
    ctx_index = lax.axis_index("ctx")
    group_extent = QUERY_HEADS // KEY_VALUE_HEADS
    kv_width = new_keys_values.shape[3]
    queries_flat = queries.reshape(1, tok_dev, queries.shape[3])
    grouped = lax.all_to_all(queries_flat, "ctx", split_axis=2, concat_axis=0, tiled=True)
    heads_here = grouped.shape[2] // HEAD_SIZE
    local_query = grouped.reshape(tok_rows, heads_here, HEAD_SIZE)
    gathered_kv, gathered_past = (
        lax.all_gather(new_keys_values.reshape(1, tok_dev, kv_width), "ctx", axis=0, tiled=True),
        lax.all_gather(
            cached_keys_values.reshape(1, past_dev, kv_width), "ctx", axis=0, tiled=True
        ),
    )
    common_key_head = ctx_index * heads_here // group_extent

    def own_head(gathered_rows):
        key_portion = lax.dynamic_slice_in_dim(
            gathered_rows, common_key_head * HEAD_SIZE, HEAD_SIZE, 2
        )
        value_portion = lax.dynamic_slice_in_dim(
            gathered_rows, KEY_VALUE_HEADS * HEAD_SIZE + common_key_head * HEAD_SIZE, HEAD_SIZE, 2
        )
        return jnp.concatenate([key_portion, value_portion], axis=2)

    own_keys = own_head(gathered_kv)
    own_past = own_head(gathered_past)
    stacked = own_keys.reshape(tok_rows, 2 * HEAD_SIZE)
    stacked_past = own_past.reshape(past_rows, 2 * HEAD_SIZE)
    keys_all = jnp.concatenate([stacked_past[:, :HEAD_SIZE], stacked[:, :HEAD_SIZE]], axis=0)
    values_all = jnp.concatenate([stacked_past[:, HEAD_SIZE:], stacked[:, HEAD_SIZE:]], axis=0)
    key_places = jnp.arange(past_rows + tok_rows) - past_rows
    block_rows = min(512, tok_rows)
    block_count = tok_rows // block_rows
    query_blocks = local_query.reshape(block_count, block_rows, heads_here, HEAD_SIZE)

    def attend(operands):
        query_block, block_index = operands
        row_places = block_index * block_rows + jnp.arange(block_rows)
        visible = (key_places[None, :] <= row_places[:, None])[:, None, :]
        scores = jnp.einsum(
            "rhd,kd->rhk", query_block, keys_all, preferred_element_type=jnp.float32
        ) * HEAD_SIZE ** (-0.5)
        scores = jnp.where(visible, scores, NEG_FILL)
        row_max = jnp.max(scores, axis=2, keepdims=True)
        weights = jnp.where(visible, jnp.exp(scores - row_max), 0.0)
        totals = jnp.sum(weights, axis=2)
        numerator = jnp.einsum(
            "rhk,kd->rhd",
            weights.astype(jnp.bfloat16),
            values_all,
            preferred_element_type=jnp.float32,
        )
        return (numerator / totals[:, :, None]).astype(jnp.bfloat16)

    attended = lax.map(attend, (query_blocks, jnp.arange(block_count)))
    head_width = heads_here * HEAD_SIZE
    attended_rows = attended.reshape(1, tok_rows, head_width)
    full_weight = lax.all_gather(out_weight, "exp", axis=0, tiled=True)
    piece = lax.all_gather(attended_rows, "ctx", axis=0, tiled=True)
    count = piece.shape[0]
    projected = jnp.einsum(
        "krc,kcd->rd",
        piece,
        full_weight.reshape(count, head_width, width_block),
        preferred_element_type=jnp.float32,
    )
    mixed = residual.reshape(tok_rows, width_block).astype(jnp.float32) + projected
    square_sum = lax.psum(jnp.sum(mixed * mixed, axis=1), "ctx")
    normed = (mixed * lax.rsqrt(square_sum / D + 1e-06)[:, None] * norm_gain[None, :]).astype(
        jnp.bfloat16
    )
    route_rows = routes.reshape(tok_rows, routes.shape[3])
    gate_rows = gates.reshape(tok_rows, gates.shape[3])
    resident = route_rows < experts_here
    has_expert = jnp.any(resident, axis=1)
    target = jnp.sum(jnp.where(resident, route_rows, 0), axis=1)
    gate_share = jnp.sum(jnp.where(resident, gate_rows, 0.0), axis=1)
    capacity = tok_rows // (2 * experts_here)
    one_hot = ((target[:, None] == jnp.arange(experts_here)[None, :]) & has_expert[:, None]).astype(
        jnp.int32
    )
    earlier_positions = jnp.cumsum(one_hot, axis=0) - one_hot
    place_index = jnp.where(
        has_expert, target * capacity + jnp.sum(earlier_positions * one_hot, axis=1), -1
    )
    placement = (place_index[None, :] == jnp.arange(experts_here * capacity)[:, None]).astype(
        jnp.bfloat16
    )
    outgoing_rows = jnp.dot(placement, normed, preferred_element_type=jnp.float32).astype(
        jnp.bfloat16
    )
    arrived = lax.all_to_all(
        outgoing_rows.reshape(experts_here, capacity, width_block),
        "exp",
        split_axis=0,
        concat_axis=0,
        tiled=True,
    )
    arrived = arrived.reshape(experts_here * capacity, width_block)
    partials = jnp.dot(arrived, w_gate_up[0], preferred_element_type=jnp.float32)
    summed = lax.psum(partials.astype(jnp.bfloat16), "ctx").astype(jnp.float32)
    activated = (jax.nn.silu(summed[:, :hidden]) * summed[:, hidden:]).astype(jnp.bfloat16)
    expert_out = jnp.dot(activated, w_down[0], preferred_element_type=jnp.float32).astype(
        jnp.bfloat16
    )
    returned = lax.all_to_all(
        expert_out.reshape(experts_here, capacity, width_block),
        "exp",
        split_axis=0,
        concat_axis=0,
        tiled=True,
    )
    collected = jnp.einsum(
        "mr,md->rd",
        placement,
        returned.reshape(experts_here * capacity, width_block),
        preferred_element_type=jnp.float32,
    )
    result = mixed + gate_share[:, None] * collected
    return result.astype(jnp.bfloat16).reshape(groups, 1, tok_dev, width_block)


def solution(mesh):
    in_specs = (
        P("ctx", "exp", None, None),
        P("ctx", "exp", None, None),
        P("ctx", "exp", None, None),
        P(None, "exp", None, "ctx"),
        P("exp", "ctx"),
        P("ctx"),
        P(None, "exp", None, None),
        P(None, "exp", None, None),
        P("exp", "ctx", None),
        P("exp", None, "ctx"),
    )
    out_specs = P(None, "exp", None, "ctx")
    return jax.shard_map(body, mesh=mesh, in_specs=in_specs, out_specs=out_specs, check_vma=False)
```

profile of v0, /device:TPU:1, one launch (start us, length us, event | category | flops | bytes accessed | tf_op | source)
XLA Modules:
  0.0 1066.8 jit_solution(7468308807224395283)
XLA Ops:
  8.0 5.3 copy.26
  13.8 23.4 %reduce.6 = bf16[4096,64]{1,0:T(8,128)(2,1)S(1)} reduce(bf16[4096,1,64]{2,1,0:T(2,128)(2,1)} %bitcast.110, bf16[]{:T(256)} %broadcast.81), dimensions={1}, to_apply=%bitcast.81.reduce_sub_computation | reduce | bytes 1048578
  38.8 19.2 %all-to-all-start = ((bf16[16,2,8192]{2,1,0:T(2,128)(2,1)}), bf16[16,2,8192]{2,1,0:T(2,128)(2,1)S(1)}, u32[]{:S(2)}, u32[]{:S(2)}) async-start(bf16[16,2,8192]{2,1,0:T(2,128)(2,1)} %reshape.149), calls=%async_computation | async-start | bytes 1048576 | tf_op jit(solution)/shard_map/all_to_all | solution.py:39
  59.0 33.3 %all-gather.11.cloned.1.call-done = bf16[16,1,64,512]{3,2,1,0:T(8,128)(2,1)} async-done(((bf16[1,1,64,512]{3,2,1,0:T(8,128)(2,1)}), bf16[16,1,64,512]{3,2,1,0:T(8,128)(2,1)}) %all-gather.11.cloned.1.call-update) | async-done | bytes 1048592 | tf_op jit(solution)/shard_map/all_gather | solution.py:44
  92.4 92.5 %all-gather.13.cloned.1.call-done = bf16[16,1,64,512]{3,2,1,0:T(8,128)(2,1)} async-done(((bf16[1,1,64,512]{3,2,1,0:T(8,128)(2,1)}), bf16[16,1,64,512]{3,2,1,0:T(8,128)(2,1)}) %all-gather.13.cloned.1.call-update) | async-done | bytes 1048592 | tf_op jit(solution)/shard_map/all_gather | solution.py:43
  187.1 3.6 reshape.150
  190.7 4.6 copy.27
  198.4 28.3 %while.11 = (s32[]{:T(128)}, bf16[2,512,2,128]{3,2,1,0:T(2,128)(2,1)}, s32[2]{0:T(128)S(1)}, bf16[2,512,2,128]{3,2,1,0:T(2,128)(2,1)S(1)}, bf16[2048,128]{1,0:T(...) while((s32[]{:T(128)}, bf16[2,512,2,128]{3,2,1,0:T(2,128)(2,1)}, ...), condition=%wide.region_3.4_spmd.clone, body=%wide.region_0.3_spmd.clone.sunk | while | flops 1087640064 | bytes 17330352 | solution.py:89
  200.5 7.2 fusion.77
  207.8 3.6 fusion.78
  214.7 7.2 fusion.77
  221.9 3.6 fusion.78
  229.3 9.0 reduce-window.6
  238.9 145.9 %all-gather.9.cloned.1.call-done = bf16[4096,256]{1,0:T(8,128)(2,1)} async-done(((bf16[128,256]{1,0:T(8,128)(2,1)}), bf16[4096,256]{1,0:T(8,128)(2,1)}) %all-gather.9.cloned.1.call-update) | async-done | bytes 2097168 | tf_op jit(solution)/shard_map/all_gather | solution.py:92
  384.8 201.9 %all-gather.7.cloned.1.call-done = bf16[16,1024,256]{2,1,0:T(8,128)(2,1)} async-done(((bf16[1,1024,256]{2,1,0:T(8,128)(2,1)}), bf16[16,1024,256]{2,1,0:T(8,128)(2,1)}) %all-gather.7.cloned.1.call-update) | async-done | bytes 8388624 | tf_op jit(solution)/shard_map/all_gather | solution.py:93
  586.8 6.5 multiply_reduce_fusion
  593.2 61.6 %psum.14 = f32[1024]{0:T(1024)S(1)} all-reduce(f32[1024]{0:T(1024)S(1)} %get-tuple-element.97), channel_id=1, replica_groups=mesh['ctx'=16,'exp'=32] {'ctx'}, use_global_device_ids=true, to_apply=%region_11.12 | all-reduce | flops 1024 | bytes 8192 | tf_op jit(solution)/shard_map/psum | solution.py:102
  655.5 19.6 %all_to_all.25 = bf16[32,16,256]{2,1,0:T(8,128)(2,1)S(1)} all-to-all(bf16[32,16,256]{2,1,0:T(8,128)(2,1)S(1)} %bitcast.119), channel_id=1, replica_groups=mesh['ctx'=16,'exp'=32] {'exp'}, dimensions={0} | all-to-all | bytes 524288 | tf_op jit(solution)/shard_map/all_to_all | solution.py:126
  675.1 2.7 convolution_convert_fusion
  677.8 351.0 %all-reduce.2.cloned.1.call-done = bf16[512,3072]{1,0:T(8,128)(2,1)} async-done(((bf16[512,3072]{1,0:T(8,128)(2,1)}), bf16[512,3072]{1,0:T(8,128)(2,1)}) %all-reduce.2.cloned.1.call-update) | async-done | bytes 3145744 | tf_op jit(solution)/shard_map/psum | solution.py:135
  1028.9 2.7 convert_element_type.48
  1033.3 9.4 all-to-all-start.2
  1042.8 14.8 %all-to-all-done.2 = bf16[32,16,256]{2,1,0:T(8,128)(2,1)S(1)} async-done(((bf16[32,16,256]{2,1,0:T(8,128)(2,1)}), bf16[32,16,256]{2,1,0:T(8,128)(2,1)S(1)}, u32[]{:S(2)}, u32[]{:S(2)}) %all-to-all-start.2) | async-done | bytes 262176 | tf_op jit(solution)/shard_map/all_to_all | solution.py:140
  1057.5 2.8 fusion.39
  (79 shorter events, 20.4 us)
Async XLA Ops:
  6.5 668.6 %copy-start = (bf16[1,256,3072]{2,1,0:T(8,128)(2,1)S(1)}, bf16[1,256,3072]{2,1,0:T(8,128)(2,1)}, u32[]{:S(2)}) copy-start(bf16[1,256,3072]{2,1,0:T(8,128)(2,1)} %param.20) | copy-start | bytes 4718596
  6.5 85.8 %all-gather.11.cloned.1.call-start = ((), (), s32[]{:S(2)}) async-start(), calls=%async_computation.6 | async-start | bytes 1114112 | tf_op jit(solution)/shard_map/all_gather | solution.py:44
  7.3 177.6 %all-gather.13.cloned.1.call-start = ((), (), s32[]{:S(2)}) async-start(), calls=%async_computation.7 | async-start | bytes 1114112 | tf_op jit(solution)/shard_map/all_gather | solution.py:43
  38.8 148.3 %all-to-all-start = ((bf16[16,2,8192]{2,1,0:T(2,128)(2,1)}), bf16[16,2,8192]{2,1,0:T(2,128)(2,1)S(1)}, u32[]{:S(2)}, u32[]{:S(2)}) async-start(bf16[16,2,8192]{2,1,0:T(2,128)(2,1)} %reshape.149), calls=%async_computation | async-start | bytes 1048576 | tf_op jit(solution)/shard_map/all_to_all | solution.py:39
  58.0 326.8 %all-gather.9.cloned.1.call-start = ((), (), s32[]{:S(2)}) async-start(), calls=%async_computation.4 | async-start | bytes 2162688 | tf_op jit(solution)/shard_map/all_gather | solution.py:92
  58.8 528.0 %all-gather.7.cloned.1.call-start = ((), (), s32[]{:S(2)}) async-start(), calls=%async_computation.3 | async-start | bytes 8912896 | tf_op jit(solution)/shard_map/all_gather | solution.py:93
  198.4 30.5 %copy-start.1 = (s32[16,1,64,8]{2,3,1,0:T(8,128)S(1)}, s32[16,1,64,8]{2,3,1,0:T(8,128)}, u32[]{:S(2)}) copy-start(s32[16,1,64,8]{2,3,1,0:T(8,128)} %param.18) | copy-start | bytes 98308
  207.8 3.6 copy-start.2
  211.7 0.8 copy-start.3
  221.9 3.6 copy-start.2
  225.8 0.8 copy-start.3
  228.9 800.0 %all-reduce.2.cloned.1.call-start = ((), (), s32[]{:S(2)}) async-start(), calls=%async_computation.5 | async-start | bytes 6291456 | tf_op jit(solution)/shard_map/psum | solution.py:135
  586.8 68.1 %copy-start.6 = (f32[256]{0:T(256)S(1)}, f32[256]{0:T(256)}, u32[]{:S(2)}) copy-start(f32[256]{0:T(256)} %param.17) | copy-start | bytes 3076
  593.2 84.6 %copy-start.7 = (f32[1024,256]{1,0:T(8,128)}, f32[1024,256]{1,0:T(8,128)S(1)}, u32[]{:S(2)}) copy-start(f32[1024,256]{1,0:T(8,128)S(1)} %get-tuple-element.98) | copy-start | bytes 3145732
  677.8 353.7 %copy-start.5 = (bf16[1,1536,256]{2,1,0:T(8,128)(2,1)S(1)}, bf16[1,1536,256]{2,1,0:T(8,128)(2,1)}, u32[]{:S(2)}) copy-start(bf16[1,1536,256]{2,1,0:T(8,128)(2,1)} %param.21) | copy-start | bytes 2359300
  1031.6 11.1 %copy-start.4 = (f32[16,1,64,8]{2,3,1,0:T(8,128)S(1)}, f32[16,1,64,8]{2,3,1,0:T(8,128)}, u32[]{:S(2)}) copy-start(f32[16,1,64,8]{2,3,1,0:T(8,128)} %param.19) | copy-start | bytes 98308
  1033.3 24.2 %all-to-all-start.2 = ((bf16[32,16,256]{2,1,0:T(8,128)(2,1)}), bf16[32,16,256]{2,1,0:T(8,128)(2,1)S(1)}, u32[]{:S(2)}, u32[]{:S(2)}) async-start(bf16[32,16,256]{2,1,0:T(8,128)(2,1)} %bitcast.17), calls=%async_computation.2 | async-start | bytes 524288 | tf_op jit(solution)/shard_map/all_to_all | solution.py:140
Sparse Core Ops, SparseCore 0:
  10.6 81.6 all-gather.10
  95.6 89.1 all-gather.12
  186.9 197.8 all-gather.8
  387.9 198.7 all-gather.6
  677.9 350.8 all-reduce.1
where the time goes:
time: 1070 us
  waiting for transfers between devices  842 us (79%)
  blocking collectives  81.2 us (8%)
  other arithmetic  39.5 us (4%)
  matrix products  35.9 us (3%)
  starting transfers between devices  28.9 us (3%)
  local copies, waits for them, and re-layouts  24.8 us (2%)
  between operations  13.4 us (1%)
    psum x1, waiting for transfers between devices, body(): summed = lax.psum(partials.astype(jnp.bfloat16), 'ctx').astype(jnp.float32)  351 us
    all_gather x1, waiting for transfers between devices, body(): piece = lax.all_gather(attended_rows, 'ctx', axis=0, tiled=True)  202 us
    all_gather x1, waiting for transfers between devices, body(): full_weight = lax.all_gather(out_weight, 'exp', axis=0, tiled=True)  146 us
    all_gather x1, waiting for transfers between devices, body(): lax.all_gather(new_keys_values.reshape(1, tok_dev, kv_width), 'ctx', axis...  92.5 us
    psum x1, blocking collectives, body(): square_sum = lax.psum(jnp.sum(mixed * mixed, axis=1), 'ctx')  61.6 us
    all_gather x1, waiting for transfers between devices, body(): lax.all_gather(cached_keys_values.reshape(1, past_dev, kv_width), 'ctx',...  33.3 us
    unnamed x1, other arithmetic  23.4 us
  transfers between devices with their start and end apart: 7, of which 6 were waited for; matrix products, arithmetic and copies ran while one was open for 8% of the time, Pallas kernels for 0%

commit v1 on v0

v1 whole, which is shorter than its diff:
```python
import math

import jax
import jax.numpy as jnp
from jax import lax
from jax.experimental import pallas as pl
from jax.experimental.pallas import tpu as pltpu
from jax.sharding import PartitionSpec as P

D = 4096
HEADS = 32
KV_HEADS = 2
HEAD = 128
FF = 1536
HALF = FF // 2
EXT = 128
NY, NX, NZ = 4, 4, 8
CH = 4
NEG = -1e30
SCALE = HEAD ** (-0.5) * math.log2(math.e)
BF = jnp.bfloat16
F32 = jnp.float32
MESH = pl.DeviceIdType.MESH


class Place:
    def __init__(self):
        ctx = lax.axis_index("ctx")
        exp = lax.axis_index("exp")
        self.y = lax.div(ctx, 4)
        self.h = lax.rem(lax.div(ctx, 2), 2)
        self.c = lax.rem(ctx, 2)
        self.x = lax.div(exp, NZ)
        self.z = lax.rem(exp, NZ)
        self.ctx = ctx
        self.exp = exp

    def dev(self, y=None, h=None, c=None, x=None, z=None):
        y = self.y if y is None else y
        h = self.h if h is None else h
        c = self.c if c is None else c
        x = self.x if x is None else x
        z = self.z if z is None else z
        return ((y * 2 + h) * 2 + c, x * NZ + z)


def rem(a, n):
    return lax.rem(a + n, n)


def send(src, dst, ss, rs, dev):
    return pltpu.make_async_remote_copy(
        src_ref=src, dst_ref=dst, send_sem=ss, recv_sem=rs, device_id=dev, device_id_type=MESH
    )


def greet(devs):
    barrier = pltpu.get_barrier_semaphore()
    for dev in devs:
        pl.semaphore_signal(barrier, inc=1, device_id=dev, device_id_type=MESH)


def loop(n, body, start=0):
    lax.fori_loop(start, n, lambda i, _: (body(i), None)[1], None)


def front_kernel(
    q_ref, new_ref, past_ref, w_ref, res_ref, mixed_ref,
    kv, wb, att, psend, precv, s_ref,
    kv_s, kv_r, wz_s, wz_r, wx_s, wx_r, at_s, at_r, p_s, p_r,
):
    me = Place()
    mate = me.dev(h=1 - me.h)
    sib = me.dev(c=1 - me.c)
    ring = me.h * NZ + me.z

    def ring_dev(step):
        there = rem(ring + step, 2 * NZ)
        return me.dev(h=lax.div(there, NZ), z=lax.rem(there, NZ))

    right, left = ring_dev(1), ring_dev(-1)
    ys = [me.dev(y=rem(me.y + k, NY)) for k in (1, 2, 3)]
    xs = [me.dev(x=rem(me.x + k, NX)) for k in (1, 2, 3)]
    greet([mate, sib, right, left] + ys + xs)

    kv[0, me.ctx] = past_ref[...]
    kv[1, me.ctx] = new_ref[...]
    wb[me.h, me.exp] = w_ref[...]
    pl.semaphore_wait(pltpu.get_barrier_semaphore(), 10)

    def kv_copy(block, slot, dev):
        part = kv.at[:, block]
        return send(part, part, kv_s.at[slot], kv_r.at[block], dev)

    def blk(y, h, c):
        return (y * 2 + h) * 2 + c

    kv_copies = []

    def kv_go(block, slot, dev):
        copy = kv_copy(block, slot, dev)
        copy.start()
        kv_copies.append(copy)

    kv_go(me.ctx, 0, mate)
    for k in (1, 2, 3):
        kv_go(me.ctx, k, ys[k - 1])
    kv_go(me.ctx, 4, sib)

    def w_part(shard, x):
        return wb.at[lax.div(shard, NZ), x * NZ + lax.rem(shard, NZ)]

    def w_right(step):
        shard = rem(ring - step + 1, 2 * NZ)
        part = w_part(shard, me.x)
        return send(part, part, wz_s.at[0, step - 1], wz_r.at[shard], right)

    def w_left(step):
        shard = rem(ring + step - 1, 2 * NZ)
        part = w_part(shard, me.x)
        return send(part, part, wz_s.at[1, step - 1], wz_r.at[shard], left)

    def w_wait(shard):
        part = w_part(shard, me.x)
        send(part, part, wz_s.at[0, 0], wz_r.at[shard], right).wait_recv()

    def w_x(shard, k):
        part = w_part(shard, me.x)
        return send(part, part, wx_s.at[k - 1, shard], wx_r.at[k - 1, shard], xs[k - 1])

    def w_spread(shard):
        for k in (1, 3, 2):
            w_x(shard, k).start()

    def ring_step(step):
        w_right(step).start()

        @pl.when(step < NZ)
        def _():
            w_left(step).start()

        one = rem(ring - step, 2 * NZ)
        w_wait(one)
        w_spread(one)

        @pl.when(step < NZ)
        def _():
            other = rem(ring + step, 2 * NZ)
            w_wait(other)
            w_spread(other)

    w_spread(ring)
    loop(3, ring_step, 1)
    for k in (1, 2, 3):
        block = blk(rem(me.y - k, NY), me.h, me.c)
        kv_copy(block, 0, sib).wait_recv()
        kv_go(block, 4 + k, sib)
    loop(6, ring_step, 3)
    block = blk(me.y, 1 - me.h, me.c)
    kv_copy(block, 0, sib).wait_recv()
    for k in (1, 2, 3):
        kv_go(block, 7 + k, ys[k - 1])
    kv_go(block, 11, sib)
    loop(NZ + 1, ring_step, 6)
    for k in (1, 2, 3):
        block = blk(rem(me.y - k, NY), 1 - me.h, me.c)
        kv_copy(block, 0, sib).wait_recv()
        kv_go(block, 11 + k, sib)
    for y in range(NY):
        for h in range(2):
            kv_copy(blk(y, h, 1 - me.c), 0, sib).wait_recv()

    mine = me.y * 2 + me.c
    tok = q_ref.shape[1]
    keys = 512

    def att_copy(chunk, who, slot, dev):
        part = att.at[chunk, who]
        return send(part, part, at_s.at[chunk, slot], at_r.at[chunk, who], dev)

    def pass_on(chunk):
        for k in (1, 2, 3):
            who = rem(me.y - k, NY) * 2 + me.c
            att_copy(chunk, who, 0, sib).wait_recv()
            att_copy(chunk, who, 3 + k, sib).start()

    def attend(chunk):
        row = lax.broadcasted_iota(jnp.int32, (tok, keys), 0)
        col = lax.broadcasted_iota(jnp.int32, (tok, keys), 1)
        last = me.ctx * 64 + chunk * tok
        for g in range(KV_HEADS):
            per = HEADS // KV_HEADS
            q = jnp.concatenate(
                [q_ref[chunk, :, (g * per + i) * HEAD : (g * per + i + 1) * HEAD] for i in range(per)], axis=0
            )
            top = None
            for kt in range(4):
                k = kv[kt // 2, (kt % 2) * 8 : (kt % 2) * 8 + 8, :, g * HEAD : (g + 1) * HEAD].reshape(keys, HEAD)
                s = lax.dot_general(q, k, (((1,), (1,)), ((), ())), preferred_element_type=F32)
                if kt >= 2:
                    bias = jnp.where(col + (kt - 2) * keys <= row + last, 0.0, NEG)
                    s = (s.reshape(per, tok, keys) + bias[None]).reshape(per * tok, keys)
                s_ref[:, kt * keys : (kt + 1) * keys] = s
                m = jnp.max(s, axis=1, keepdims=True)
                top = m if top is None else jnp.maximum(top, m)
            total = None
            acc = None
            for kt in range(4):
                p = jnp.exp2((s_ref[:, kt * keys : (kt + 1) * keys] - top) * SCALE)
                v = kv[
                    kt // 2, (kt % 2) * 8 : (kt % 2) * 8 + 8, :, (KV_HEADS + g) * HEAD : (KV_HEADS + g + 1) * HEAD
                ].reshape(keys, HEAD)
                t = jnp.sum(p, axis=1, keepdims=True)
                o = jnp.dot(p.astype(BF), v, preferred_element_type=F32)
                total = t if total is None else total + t
                acc = o if acc is None else acc + o
            out = (acc / total).astype(BF)
            for i in range(per):
                att[chunk, mine, :, (g * per + i) * HEAD : (g * per + i + 1) * HEAD] = out[i * tok : (i + 1) * tok]
        for k in (1, 2, 3):
            att_copy(chunk, mine, k - 1, ys[k - 1]).start()
        att_copy(chunk, mine, 3, sib).start()

        @pl.when(chunk > 0)
        def _():
            pass_on(chunk - 1)

    loop(CH, attend)
    pass_on(CH - 1)

    def w_arrive(shard):
        for k in (1, 2, 3):
            part = w_part(shard, rem(me.x - k, NX))
            send(part, part, wx_s.at[k - 1, shard], wx_r.at[k - 1, shard], xs[k - 1]).wait_recv()

    loop(2 * NZ, w_arrive)

    def p_copy(chunk):
        return send(psend.at[chunk], precv.at[chunk], p_s.at[chunk], p_r.at[chunk], mate)

    def rows_of(chunk):
        return att[chunk].reshape(8 * tok, D)

    def for_mate(chunk):
        for y in range(NY):
            att_copy(chunk, y * 2 + 1 - me.c, 0, sib).wait_recv()
        w = wb[1 - me.h].reshape(D, 256)
        psend[chunk] = jnp.dot(rows_of(chunk), w, preferred_element_type=F32).astype(BF)
        p_copy(chunk).start()

    loop(CH, for_mate)

    def place(chunk, half, value):
        for j in range(8):
            block = (j // 2) * 4 + half * 2 + j % 2
            mixed_ref[block, chunk] = res_ref[block, chunk].astype(F32) + value[j * tok : (j + 1) * tok].astype(F32)

    def for_me(chunk):
        w = wb[me.h].reshape(D, 256)
        place(chunk, me.h, jnp.dot(rows_of(chunk), w, preferred_element_type=F32))

    loop(CH, for_me)

    def from_mate(chunk):
        p_copy(chunk).wait_recv()
        place(chunk, 1 - me.h, precv[chunk])

    loop(CH, from_mate)

    for copy in kv_copies:
        copy.wait_send()

    def ring_left(step):
        w_right(step).wait_send()

        @pl.when(step < NZ)
        def _():
            w_left(step).wait_send()

    loop(NZ + 1, ring_left, 1)

    def x_left(shard):
        for k in (1, 2, 3):
            w_x(shard, k).wait_send()

    loop(2 * NZ, x_left)

    def att_left(chunk):
        for slot in range(7):
            att_copy(chunk, mine, slot, sib).wait_send()
        p_copy(chunk).wait_send()

    loop(CH, att_left)


def front(queries, new, past, w, res):
    sem = pltpu.SemaphoreType.DMA
    return pl.pallas_call(
        front_kernel,
        out_shape=jax.ShapeDtypeStruct((16, CH, 16, 256), F32),
        in_specs=[pl.BlockSpec(memory_space=pltpu.VMEM)] * 5,
        out_specs=pl.BlockSpec(memory_space=pltpu.VMEM),
        scratch_shapes=[
            pltpu.VMEM((2, 16, 64, 512), BF),
            pltpu.VMEM((2, 32, 128, 256), BF),
            pltpu.VMEM((CH, 8, 16, D), BF),
            pltpu.VMEM((CH, 128, 256), BF),
            pltpu.VMEM((CH, 128, 256), BF),
            pltpu.VMEM((256, 2048), F32),
            sem((15,)), sem((16,)),
            sem((2, 8)), sem((16,)),
            sem((3, 16)), sem((3, 16)),
            sem((CH, 7)), sem((CH, 8)),
            sem((CH,)), sem((CH,)),
        ],
        compiler_params=pltpu.CompilerParams(
            collective_id=0, has_side_effects=True, vmem_limit_bytes=48 * 2**20
        ),
        name="front",
    )(queries, new, past, w, res)


def pieces(column, rows):
    lane = lax.broadcasted_iota(jnp.int32, (rows, EXT), 1)
    wide = jnp.broadcast_to(column, (rows, EXT))
    high = wide.astype(BF).astype(F32)
    rest = wide - high
    middle = rest.astype(BF).astype(F32)
    low = rest - middle
    out = jnp.where(lane == 0, high, jnp.where(lane == 1, middle, jnp.where(lane == 2, low, 0.0)))
    return out.astype(BF)


def expert_kernel(
    mixed_ref, gain_ref, routes_ref, gates_ref, gu_ref, wd_ref, out_ref,
    gains, wgs, disp, arr, sarr, pb, yr, zb, zr, act, eo, rb, place_ref, share_ref,
    c_s, c_r, d_s, d_r, a_s, a_r, y_s, y_r, z_s, z_r, az_s, az_r, ay_s, ay_r, ac_s, ac_r, e_s, e_r,
):
    me = Place()
    mate = me.dev(h=1 - me.h)
    sib = me.dev(c=1 - me.c)
    ys = [me.dev(y=rem(me.y + k, NY)) for k in (1, 2, 3)]
    barrier = pltpu.get_barrier_semaphore()
    greet([mate, sib] + ys)

    def peer(o):
        x = rem(me.x + lax.div(o, NZ), NX)
        z = rem(me.z + lax.rem(o, NZ), NZ)
        return x * NZ + z

    def peer_dev(e):
        return (me.ctx, e)

    def hello(o):
        pl.semaphore_signal(barrier, inc=1, device_id=peer_dev(peer(o)), device_id_type=MESH)

    loop(NX * NZ, hello, 1)

    toks = routes_ref.shape[0]
    routes = routes_ref[...]
    held = routes < NX * NZ
    target = jnp.sum(jnp.where(held, routes, 0), axis=1, keepdims=True)
    has = jnp.sum(jnp.where(held, 1, 0), axis=1, keepdims=True)
    share_ref[...] = jnp.sum(jnp.where(held, gates_ref[...], 0.0), axis=1, keepdims=True)
    lane = lax.broadcasted_iota(jnp.int32, (toks, 128), 1)
    named = jnp.where(has > 0, target, -1)
    hot = jnp.where(lane == named, 1.0, 0.0)
    step = 128
    seen = jnp.zeros((1, 128), F32)
    tri = jnp.where(
        lax.broadcasted_iota(jnp.int32, (step, step), 1) < lax.broadcasted_iota(jnp.int32, (step, step), 0), 1.0, 0.0
    ).astype(BF)
    slot = lax.broadcasted_iota(jnp.int32, (step, 512), 1)
    for t in range(toks // step):
        part = hot[t * step : (t + 1) * step]
        before = jnp.dot(tri, part.astype(BF), preferred_element_type=F32) + seen
        at = jnp.sum(before * part, axis=1, keepdims=True).astype(jnp.int32)
        here = named[t * step : (t + 1) * step]
        index = jnp.where(here >= 0, here * 16 + at, -1)
        place_ref[t * step : (t + 1) * step] = jnp.where(slot == index, 1.0, 0.0).astype(BF)
        seen = seen + jnp.sum(part, axis=0, keepdims=True)

    gains[me.c] = jnp.broadcast_to(gain_ref[...], (8, 256))
    rows = (mixed_ref[...].reshape(toks, 256) * gain_ref[...]).astype(BF)
    picked = lax.dot_general(place_ref[...], rows, (((0,), (0,)), ((), ())), preferred_element_type=F32)
    disp[...] = picked.astype(BF).reshape(32, 16, 256)
    arr[me.exp] = disp[me.exp]
    pl.semaphore_wait(barrier, 36)

    def d_copy(o):
        e = peer(o)
        return send(disp.at[e], arr.at[me.exp], d_s.at[o], d_r.at[me.exp], peer_dev(e))

    loop(NX * NZ, lambda o: d_copy(o).start(), 1)

    theirs = pl.multiple_of((1 - me.c) * HALF, 128)
    c_copies = [
        send(gu_ref.at[:, pl.ds(theirs, HALF)], wgs.at[:, pl.ds(0, HALF)], c_s.at[0], c_r.at[0], sib),
        send(gu_ref.at[:, pl.ds(theirs + FF, HALF)], wgs.at[:, pl.ds(HALF, HALF)], c_s.at[1], c_r.at[1], sib),
        send(gains.at[me.c], gains.at[me.c], c_s.at[2], c_r.at[2], sib),
    ]
    for copy in c_copies:
        copy.start()

    def src_x(q):
        return rem(me.x - q, NX)

    def a_copy(q):
        x = src_x(q)
        part = arr.at[pl.ds(x * NZ, NZ)]
        return send(part, sarr.at[pl.ds(x * NZ, NZ)], a_s.at[x], a_r.at[x], sib)

    def collect(q):
        x = src_x(q)

        def one(z):
            e = x * NZ + z

            @pl.when(e != me.exp)
            def _():
                send(disp.at[0], arr.at[e], d_s.at[0], d_r.at[e], sib).wait_recv()

        loop(NZ, one)
        a_copy(q).start()

    loop(CH, collect)
    c_copies[0].wait_recv()
    c_copies[1].wait_recv()
    send(gains.at[me.c], gains.at[1 - me.c], c_s.at[2], c_r.at[2], sib).wait_recv()
    ours = pl.multiple_of(me.c * HALF, 128)

    def y_copy(q, k):
        there = rem(me.y + k, NY)
        part = pb.at[q, pl.ds(there * 32, 32)]
        return send(part, yr.at[q, k - 1], y_s.at[q, k - 1], y_r.at[q, k - 1], ys[k - 1])

    def gate_up(q):
        x = src_x(q)
        a_copy(q).wait_recv()
        mine = arr[pl.ds(x * NZ, NZ)].reshape(128, 256)
        other = sarr[pl.ds(x * NZ, NZ)].reshape(128, 256)
        a = mine.astype(F32) / gains[me.c, 0:1]
        b = other.astype(F32) / gains[1 - me.c, 0:1]
        squares = jnp.sum(a * a, axis=1, keepdims=True) + jnp.sum(b * b, axis=1, keepdims=True)
        pb[q, :, FF * 1 :] = pieces(squares, 128)
        gate = jnp.dot(mine, gu_ref[:, pl.ds(ours, HALF)], preferred_element_type=F32)
        gate += jnp.dot(other, wgs[:, 0:HALF], preferred_element_type=F32)
        pb[q, :, 0:HALF] = gate.astype(BF)
        up = jnp.dot(mine, gu_ref[:, pl.ds(ours + FF, HALF)], preferred_element_type=F32)
        up += jnp.dot(other, wgs[:, HALF:FF], preferred_element_type=F32)
        pb[q, :, HALF:FF] = up.astype(BF)
        for k in (1, 2, 3):
            y_copy(q, k).start()

    loop(CH, gate_up)

    def z_copy(q):
        part = zb.at[q, pl.ds((1 - me.h) * 16, 16)]
        return send(part, zr.at[q], z_s.at[q], z_r.at[q], mate)

    def y_sum(q):
        total = pb[q, pl.ds(pl.multiple_of(me.y * 32, 32), 32)].astype(F32)
        for k in (1, 2, 3):
            y_copy(q, k).wait_recv()
            total = total + yr[q, k - 1].astype(F32)
        zb[q, :, 0:FF] = total[:, 0:FF].astype(BF)
        zb[q, :, FF:] = pieces(jnp.sum(total[:, FF:], axis=1, keepdims=True), 32)
        z_copy(q).start()

    loop(CH, y_sum)

    def az_copy(q):
        part = act.at[q, me.c, me.y, me.h]
        return send(part, part, az_s.at[q], az_r.at[q], mate)

    def activate(q):
        z_copy(q).wait_recv()
        total = zb[q, pl.ds(pl.multiple_of(me.h * 16, 16), 16)].astype(F32) + zr[q].astype(F32)
        squares = jnp.sum(total[:, FF:], axis=1, keepdims=True)
        scale = lax.rsqrt(squares / D + 1e-6)
        gate = total[:, 0:HALF] * scale
        up = total[:, HALF:FF] * scale
        act[q, me.c, me.y, me.h] = (gate / (1.0 + jnp.exp(-gate)) * up).astype(BF)
        az_copy(q).start()

    loop(CH, activate)

    def ay_copy(q, y, k):
        part = act.at[q, me.c, y]
        return send(part, part, ay_s.at[q, k - 1], ay_r.at[q, y], ys[k - 1])

    def spread(q):
        part = act.at[q, me.c, me.y, 1 - me.h]
        send(part, part, az_s.at[q], az_r.at[q], mate).wait_recv()
        for k in (1, 2, 3):
            ay_copy(q, me.y, k).start()

    loop(CH, spread)

    def ac_copy(q, c):
        part = act.at[q, c]
        return send(part, part, ac_s.at[q], ac_r.at[q], sib)

    def share(q):
        for k in (1, 2, 3):
            ay_copy(q, rem(me.y - k, NY), k).wait_recv()
        ac_copy(q, me.c).start()

    loop(CH, share)

    def e_copy(o):
        e = peer(o)
        return send(eo.at[e], rb.at[me.exp], e_s.at[o], e_r.at[me.exp], peer_dev(e))

    def down(q):
        x = src_x(q)
        ac_copy(q, 1 - me.c).wait_recv()
        value = jnp.dot(act[q, 0].reshape(128, HALF), wd_ref[0:HALF], preferred_element_type=F32)
        value += jnp.dot(act[q, 1].reshape(128, HALF), wd_ref[HALF:FF], preferred_element_type=F32)
        eo[pl.ds(x * NZ, NZ)] = value.astype(BF).reshape(NZ, 16, 256)

        def back(z):
            o = rem(NX - q, NX) * NZ + z

            @pl.when(o != 0)
            def _():
                e_copy(o).start()

        loop(NZ, back)

    loop(CH, down)
    rb[me.exp] = eo[me.exp]

    def home(e):
        @pl.when(e != me.exp)
        def _():
            send(eo.at[0], rb.at[e], e_s.at[0], e_r.at[e], sib).wait_recv()

    loop(NX * NZ, home)
    back = rb[...].reshape(512, 256)
    for t in range(4):
        got = jnp.dot(place_ref[t * 256 : (t + 1) * 256], back, preferred_element_type=F32)
        value = mixed_ref[t * 4 : (t + 1) * 4].reshape(256, 256) + share_ref[t * 256 : (t + 1) * 256] * got
        out_ref[t * 4 : (t + 1) * 4] = value.astype(BF).reshape(4, 64, 256)

    for copy in c_copies:
        copy.wait_send()

    def peers_left(o):
        d_copy(o).wait_send()
        e_copy(o).wait_send()

    loop(NX * NZ, peers_left, 1)

    def chunk_left(q):
        a_copy(q).wait_send()
        z_copy(q).wait_send()
        az_copy(q).wait_send()
        ac_copy(q, me.c).wait_send()
        for k in (1, 2, 3):
            y_copy(q, k).wait_send()
            ay_copy(q, me.y, k).wait_send()

    loop(CH, chunk_left)


def experts(mixed, gain, routes, gates, gu, wd):
    sem = pltpu.SemaphoreType.DMA
    wide = FF + EXT
    return pl.pallas_call(
        expert_kernel,
        out_shape=jax.ShapeDtypeStruct((16, 64, 256), BF),
        in_specs=[pl.BlockSpec(memory_space=pltpu.VMEM)] * 6,
        out_specs=pl.BlockSpec(memory_space=pltpu.VMEM),
        scratch_shapes=[
            pltpu.VMEM((2, 8, 256), F32),
            pltpu.VMEM((256, FF), BF),
            pltpu.VMEM((32, 16, 256), BF),
            pltpu.VMEM((32, 16, 256), BF),
            pltpu.VMEM((32, 16, 256), BF),
            pltpu.VMEM((CH, 128, wide), BF),
            pltpu.VMEM((CH, 3, 32, wide), BF),
            pltpu.VMEM((CH, 32, wide), BF),
            pltpu.VMEM((CH, 16, wide), BF),
            pltpu.VMEM((CH, 2, NY, 2, 16, HALF), BF),
            pltpu.VMEM((32, 16, 256), BF),
            pltpu.VMEM((32, 16, 256), BF),
            pltpu.VMEM((1024, 512), BF),
            pltpu.VMEM((1024, 1), F32),
            sem((3,)), sem((3,)),
            sem((32,)), sem((32,)),
            sem((4,)), sem((4,)),
            sem((CH, 3)), sem((CH, 3)),
            sem((CH,)), sem((CH,)),
            sem((CH,)), sem((CH,)),
            sem((CH, 3)), sem((CH, NY)),
            sem((CH,)), sem((CH,)),
            sem((32,)), sem((32,)),
        ],
        compiler_params=pltpu.CompilerParams(
            collective_id=1, has_side_effects=True, vmem_limit_bytes=48 * 2**20
        ),
        name="experts",
    )(mixed, gain, routes, gates, gu, wd)


def body(queries, new_kv, past_kv, residual, out_weight, norm_gain, routes, gates, w_gate_up, w_down):
    mixed = front(
        queries.reshape(CH, 16, D),
        new_kv.reshape(64, 512),
        past_kv.reshape(64, 512),
        out_weight,
        residual.reshape(16, CH, 16, 256),
    )
    out = experts(
        mixed.reshape(16, 64, 256),
        norm_gain.reshape(1, 256),
        routes.reshape(1024, 8),
        gates.reshape(1024, 8),
        w_gate_up.reshape(256, 2 * FF),
        w_down.reshape(FF, 256),
    )
    return out.reshape(16, 1, 64, 256)


def solution(mesh):
    in_specs = (
        P("ctx", "exp", None, None),
        P("ctx", "exp", None, None),
        P("ctx", "exp", None, None),
        P(None, "exp", None, "ctx"),
        P("exp", "ctx"),
        P("ctx"),
        P(None, "exp", None, None),
        P(None, "exp", None, None),
        P("exp", "ctx", None),
        P("exp", None, "ctx"),
    )
    return jax.shard_map(
        body, mesh=mesh, in_specs=in_specs, out_specs=P(None, "exp", None, "ctx"), check_vma=False
    )
```

time: 1070 us -> 211 us (0.20)
  waiting for transfers between devices: 842 us -> 0 us
  Pallas kernels: 0 us -> 203 us
  blocking collectives: 81.2 us -> 0 us
  other arithmetic: 39.5 us -> 0 us
  matrix products: 35.9 us -> 0 us
  starting transfers between devices: 28.9 us -> 0 us
  local copies, waits for them, and re-layouts: 24.8 us -> 7.65 us
  between operations: 13.4 us -> 0.09 us
    all_gather x4 -> x0, waiting for transfers between devices: 474 us -> none  [the longest x1 202 us: body(): piece = lax.all_gather(attended_rows, 'ctx', axis=0, tiled=True)]
    psum x1 -> x0, waiting for transfers between devices: 351 us -> none  [body(): summed = lax.psum(partials.astype(jnp.bfloat16), 'ctx').astype(jnp.float32)]
    pallas_call x0 -> x2, Pallas kernels: none -> 203 us  [the longest x1 117 us: front(): pl.pallas_call(front_kernel, out_shape=jax.ShapeDtypeStruct((16, CH, 16,...]
    psum x1 -> x0, blocking collectives: 61.6 us -> none  [body(): square_sum = lax.psum(jnp.sum(mixed * mixed, axis=1), 'ctx')]
    all_to_all x2 -> x0, starting transfers between devices: 28.6 us -> none  [the longest x1 19.2 us: body(): lax.all_to_all(queries_flat, 'ctx', split_axis=2, concat_axis=0, tiled=True)]
    unnamed x1 -> x0, other arithmetic: 23.4 us -> none
    dot_general x7 -> x0, matrix products: 21.5 us -> none  [the longest x2 7.25 us: attend(): jnp.einsum('rhk,kd->rhd', weights.astype(jnp.bfloat16), values_all, prefe...]
    all_to_all x1 -> x0, blocking collectives: 19.6 us -> none  [body(): lax.all_to_all(outgoing_rows.reshape(experts_here, capacity, width_block)...]
  transfers between devices with their start and end apart: 7 -> 0, of which waited for: 6 -> 0; matrix products, arithmetic and copies ran while one was open for 8% -> 0% of each run, Pallas kernels for 0% -> 0%
where the time goes in v1:
time: 211 us
  Pallas kernels  203 us (96%)
  local copies, waits for them, and re-layouts  7.65 us (4%)
    pallas_call x1, Pallas kernels, front(): pl.pallas_call(front_kernel, out_shape=jax.ShapeDtypeStruct((16, CH, 16,...  117 us
    pallas_call x1, Pallas kernels, experts(): pl.pallas_call(expert_kernel, out_shape=jax.ShapeDtypeStruct((16, 64, 256...  86.6 us
    unnamed x19, local copies, waits for them, and re-layouts  7.65 us

profile of v1, /device:TPU:1, one launch (start us, length us, event | category | flops | bytes accessed | tf_op | source)
XLA Modules:
  0.0 211.0 jit_solution(8836304748728457619)
XLA Ops:
  0.0 0.0 copy-start.7
  0.0 1.1 copy.11
  1.1 0.0 copy-start
  1.1 0.0 copy-start.1
  1.1 1.2 copy.12
  2.3 0.0 copy-start.2
  2.3 1.0 copy-done.2
  3.3 0.0 copy-start.3
  3.3 1.0 copy-done.3
  4.4 0.0 copy-start.4
  4.4 0.8 copy-done.4
  5.2 0.0 copy-start.5
  5.2 0.8 copy-done.5
  6.1 0.0 copy-start.6
  6.1 0.8 copy-done.6
  6.9 116.7 %front.1 = f32[16,4,16,256]{3,2,1,0:T(8,128)S(1)} custom-call(bf16[4,16,4096]{2,1,0:T(8,128)(2,1)S(1)} %bitcast.19, bf16[64,512]{1,0:T(8,128)(2,1)S(1)} %bitcast.21, bf16[64,512]{1,0:T(8,128)(2,1)S(1)} %bitcast.22, bf16[128,256]{1,0:T(8,128)(2,1)S(1)} %copy-done.6, bf16[16,4,16,256]{3,2,1,0:T(8,128)(2,1)S(1)} %bitcast.20), custom_call_target="tpu_custom_call" | custom-call | tf_op jit(solution)/shard_map/front/pallas_call | solution.py:298
  123.6 0.0 copy-done.7
  123.6 0.0 copy-done
  123.6 0.0 copy-done.1
  123.6 86.6 %experts.1 = bf16[16,64,256]{2,1,0:T(8,128)(2,1)S(1)} custom-call(f32[16,64,256]{2,1,0:T(8,128)S(1)} %bitcast.13, f32[1,256]{1,0:T(1,128)S(1)} %bitcast.23, s32[1024,8]{1,0:T(8,128)S(1)} %bitcast.15, f32[1024,8]{1,0:T(8,128)S(1)} %bitcast.16, bf16[256,3072]{1,0:T(8,128)(2,1)S(1)} %bitcast.17, bf16[1536,256]{1,0:T(8,128)(2,1)S(1)} %bitcast.18), custom_call_target="tpu_custom_call" | custom-call | tf_op jit(solution)/shard_map/experts/pallas_call | solution.py:570
  210.2 0.8 copy.15
Async XLA Ops:
  0.0 123.6 %copy-start.7 = (f32[256]{0:T(256)S(1)}, f32[256]{0:T(256)}, u32[]{:S(2)}) copy-start(f32[256]{0:T(256)} %param.15) | copy-start | bytes 3076
  1.1 122.5 %copy-start = (bf16[1,256,3072]{2,1,0:T(8,128)(2,1)S(1)}, bf16[1,256,3072]{2,1,0:T(8,128)(2,1)}, u32[]{:S(2)}) copy-start(bf16[1,256,3072]{2,1,0:T(8,128)(2,1)} %param.18) | copy-start | bytes 4718596
  1.1 122.5 %copy-start.1 = (bf16[1,1536,256]{2,1,0:T(8,128)(2,1)S(1)}, bf16[1,1536,256]{2,1,0:T(8,128)(2,1)}, u32[]{:S(2)}) copy-start(bf16[1,1536,256]{2,1,0:T(8,128)(2,1)} %param.19) | copy-start | bytes 2359300
  2.3 1.0 copy-start.2
  3.3 1.0 copy-start.3
  4.4 0.8 copy-start.4
  5.2 0.8 copy-start.5
  6.1 0.8 copy-start.6

commit v2 on v1

v2 whole, which is shorter than its diff:
```python
import math

import jax
import jax.numpy as jnp
from jax import lax
from jax.experimental import pallas as pl
from jax.experimental.pallas import tpu as pltpu
from jax.sharding import PartitionSpec as P

D = 4096
HEADS = 32
KV_HEADS = 2
HEAD = 128
FF = 1536
HALF = FF // 2
EXT = 128
NY, NX, NZ = 4, 4, 8
CH = 4
NEG = -1e30
SCALE = HEAD ** (-0.5) * math.log2(math.e)
BF = jnp.bfloat16
F32 = jnp.float32
MESH = pl.DeviceIdType.MESH


class Place:
    def __init__(self):
        ctx = lax.axis_index("ctx")
        exp = lax.axis_index("exp")
        self.y = lax.div(ctx, 4)
        self.h = lax.rem(lax.div(ctx, 2), 2)
        self.c = lax.rem(ctx, 2)
        self.x = lax.div(exp, NZ)
        self.z = lax.rem(exp, NZ)
        self.ctx = ctx
        self.exp = exp

    def dev(self, y=None, h=None, c=None, x=None, z=None):
        y = self.y if y is None else y
        h = self.h if h is None else h
        c = self.c if c is None else c
        x = self.x if x is None else x
        z = self.z if z is None else z
        return ((y * 2 + h) * 2 + c, x * NZ + z)


def rem(a, n):
    return lax.rem(a + n, n)


def send(src, dst, ss, rs, dev):
    return pltpu.make_async_remote_copy(
        src_ref=src, dst_ref=dst, send_sem=ss, recv_sem=rs, device_id=dev, device_id_type=MESH
    )


def greet(devs):
    barrier = pltpu.get_barrier_semaphore()
    for dev in devs:
        pl.semaphore_signal(barrier, inc=1, device_id=dev, device_id_type=MESH)


def loop(n, body, start=0):
    lax.fori_loop(start, n, lambda i, _: (body(i), None)[1], None)


def pieces(column, rows):
    lane = lax.broadcasted_iota(jnp.int32, (rows, EXT), 1)
    wide = jnp.broadcast_to(column, (rows, EXT))
    high = wide.astype(BF).astype(F32)
    rest = wide - high
    middle = rest.astype(BF).astype(F32)
    low = rest - middle
    out = jnp.where(lane == 0, high, jnp.where(lane == 1, middle, jnp.where(lane == 2, low, 0.0)))
    return out.astype(BF)


def layer_kernel(
    q_hbm, new_hbm, past_hbm, w_hbm, res_hbm, gain_hbm, routes_hbm, gates_hbm, gu_hbm, wd_hbm, out_ref,
    q_ref, kv, wb, res_ref, gain_ref, routes_ref, gates_ref, gu_ref, wd_ref,
    att, accs, tops, sums, s_ref, psend, precv, mixed, place_ref, place_t, share_ref,
    gains, wgs, picked, disp, arr, sarr, pb, yr, zb, zr, act, eo, rb,
    in_s, kv_s, kv_r, wz_s, wz_r, wx_s, wx_r, at_s, at_r, ah_r, p_s, p_r,
    c_s, c_r, d_s, d_r, a_s, a_r, y_s, y_r, z_s, z_r, az_s, az_r, ay_s, ay_r, ac_s, ac_r, e_s, e_r,
):
    me = Place()
    mate = me.dev(h=1 - me.h)
    sib = me.dev(c=1 - me.c)
    ring = me.h * NZ + me.z

    def ring_dev(step):
        there = rem(ring + step, 2 * NZ)
        return me.dev(h=lax.div(there, NZ), z=lax.rem(there, NZ))

    right, left = ring_dev(1), ring_dev(-1)
    ys = [me.dev(y=rem(me.y + k, NY)) for k in (1, 2, 3)]
    xs = [me.dev(x=rem(me.x + k, NX)) for k in (1, 2, 3)]

    def peer(o):
        x = rem(me.x + lax.div(o, NZ), NX)
        z = rem(me.z + lax.rem(o, NZ), NZ)
        return x * NZ + z

    def peer_dev(e):
        return (me.ctx, e)

    barrier = pltpu.get_barrier_semaphore()
    greet([mate, sib, right, left] + ys)

    def hello(o):
        pl.semaphore_signal(barrier, inc=1, device_id=peer_dev(peer(o)), device_id_type=MESH)

    loop(NX * NZ, hello, 1)

    pairs = [
        (past_hbm, kv.at[0, me.y, me.h, me.c]),
        (new_hbm, kv.at[1, me.y, me.h, me.c]),
        (w_hbm, wb.at[me.h, me.exp]),
        (routes_hbm, routes_ref),
        (gates_hbm, gates_ref),
        (q_hbm, q_ref),
        (gain_hbm, gain_ref),
        (gu_hbm, gu_ref),
        (wd_hbm, wd_ref),
        (res_hbm, res_ref),
    ]
    loads = [pltpu.make_async_copy(src, dst, in_s.at[i]) for i, (src, dst) in enumerate(pairs)]
    for load in loads:
        load.start()

    loads[3].wait()
    loads[4].wait()
    slots = 512
    step = 128
    tri = jnp.where(
        lax.broadcasted_iota(jnp.int32, (step, step), 1) < lax.broadcasted_iota(jnp.int32, (step, step), 0), 1.0, 0.0
    ).astype(BF)
    lane = lax.broadcasted_iota(jnp.int32, (step, 128), 1)
    slot = lax.broadcasted_iota(jnp.int32, (step, slots), 1)
    seen = jnp.zeros((1, 128), F32)

    def by_token(ref, t):
        return jnp.concatenate([ref[2 * t].T, ref[2 * t + 1].T], axis=0)

    for t in range(8):
        half, y = t % 2, t // 2
        routes = by_token(routes_ref, t)
        held = routes < NX * NZ
        target = jnp.sum(jnp.where(held, routes, 0), axis=1, keepdims=True)
        has = jnp.sum(jnp.where(held, 1, 0), axis=1, keepdims=True)
        share_ref[half, y * step : (y + 1) * step] = jnp.sum(
            jnp.where(held, by_token(gates_ref, t), 0.0), axis=1, keepdims=True
        )
        named = jnp.where(has > 0, target, -1)
        part = jnp.where(lane == named, 1.0, 0.0)
        before = jnp.dot(tri, part.astype(BF), preferred_element_type=F32) + seen
        at = jnp.sum(before * part, axis=1, keepdims=True).astype(jnp.int32)
        index = jnp.where(named >= 0, named * 16 + at, -1)
        hot = jnp.where(slot == index, 1.0, 0.0)
        place_ref[half, y * step : (y + 1) * step] = hot.astype(BF)
        place_t[half, :, y * step : (y + 1) * step] = hot.T.astype(BF)
        seen = seen + jnp.sum(part, axis=0, keepdims=True)

    for i in (0, 1, 2):
        loads[i].wait()
    pl.semaphore_wait(barrier, 38)

    def kv_copy(n, y, h, c, out, dev):
        part = kv.at[n, y, h, c]
        return send(part, part, kv_s.at[out], kv_r.at[n, y, h, c], dev)

    kv_copies = []

    def kv_go(n, y, h, c, dev):
        copy = kv_copy(n, y, h, c, len(kv_copies), dev)
        copy.start()
        kv_copies.append(copy)

    def kv_wait(n, y, h, c):
        kv_copy(n, y, h, c, 0, sib).wait_recv()

    for n in range(2):
        kv_go(n, me.y, me.h, me.c, mate)
    for n in range(2):
        for k in (0, 2, 1):
            kv_go(n, me.y, me.h, me.c, ys[k])
        kv_go(n, me.y, me.h, me.c, sib)

    def w_part(shard, x):
        return wb.at[lax.div(shard, NZ), x * NZ + lax.rem(shard, NZ)]

    def w_right(s):
        shard = rem(ring - s + 1, 2 * NZ)
        part = w_part(shard, me.x)
        return send(part, part, wz_s.at[0, s - 1], wz_r.at[shard], right)

    def w_left(s):
        shard = rem(ring + s - 1, 2 * NZ)
        part = w_part(shard, me.x)
        return send(part, part, wz_s.at[1, s - 1], wz_r.at[shard], left)

    def w_wait(shard):
        part = w_part(shard, me.x)
        send(part, part, wz_s.at[0, 0], wz_r.at[shard], right).wait_recv()

    x_up, x_down = xs[0], xs[2]

    def w_x(shard, i):
        if i < 2:
            part = w_part(shard, me.x)
        else:
            part = w_part(shard, rem(me.x + 2 * i - 5, NX)).at[pl.ds((i - 2) * 64, 64)]
        return send(part, part, wx_s.at[i, shard], wx_r.at[i, shard], (x_up, x_down)[i % 2])

    def w_x_wait(shard, i):
        part = w_part(shard, rem(me.x + (-1, 1, 2, 2)[i], NX))
        if i >= 2:
            part = part.at[pl.ds((i - 2) * 64, 64)]
        send(part, part, wx_s.at[i, shard], wx_r.at[i, shard], x_up).wait_recv()

    def w_spread(shard):
        for i in (0, 1):
            w_x(shard, i).start()

    def w_pass(shard):
        for i in (0, 1):
            w_x_wait(shard, i)
            w_x(shard, i + 2).start()

    def ring_send(s):
        w_right(s).start()

        @pl.when(s < NZ)
        def _():
            w_left(s).start()

    def ring_take(s):
        one = rem(ring - s, 2 * NZ)
        w_wait(one)

        @pl.when(s < NZ)
        def _():
            w_wait(rem(ring + s, 2 * NZ))

    def both(s, act_on):
        act_on(rem(ring - s, 2 * NZ))

        @pl.when(s < NZ)
        def _():
            act_on(rem(ring + s, 2 * NZ))

    def ring_step(s):
        ring_take(s)

        @pl.when(s < NZ)
        def _():
            ring_send(s + 1)

        both(s, w_spread)

    ring_send(1)
    w_spread(ring)
    for n in range(2):
        for k in (1, 3, 2):
            y = rem(me.y - k, NY)
            kv_wait(n, y, me.h, me.c)
            kv_go(n, y, me.h, me.c, sib)
    ring_step(1)
    for n in range(2):
        for y in range(NY):
            kv_wait(n, y, me.h, 1 - me.c)
    loads[5].wait()

    mine = me.y * 2 + me.c
    tok = 16
    keys = 512
    per = HEADS // KV_HEADS
    row = lax.broadcasted_iota(jnp.int32, (tok, keys), 0)
    col = lax.broadcasted_iota(jnp.int32, (tok, keys), 1)

    def attend(chunk, half, first):
        spot = lax.div(col, 128) * 256 + half * 128 + lax.rem(col, 128)
        bias = jnp.where(spot <= row + (me.ctx * 64 + chunk * tok), 0.0, NEG)
        for g in range(KV_HEADS):
            q = jnp.concatenate(
                [q_ref[chunk, :, (g * per + i) * HEAD : (g * per + i + 1) * HEAD] for i in range(per)], axis=0
            )
            top = None if first else tops[chunk, g]
            for kt in range(2):
                k = kv[kt, :, half, :, :, g * HEAD : (g + 1) * HEAD].reshape(keys, HEAD)
                s = lax.dot_general(q, k, (((1,), (1,)), ((), ())), preferred_element_type=F32)
                if kt == 1:
                    s = (s.reshape(per, tok, keys) + bias[None]).reshape(per * tok, keys)
                s_ref[:, kt * keys : (kt + 1) * keys] = s
                m = jnp.max(s, axis=1, keepdims=True)
                top = m if top is None else jnp.maximum(top, m)
            total = None
            acc = None
            for kt in range(2):
                p = jnp.exp2((s_ref[:, kt * keys : (kt + 1) * keys] - top) * SCALE)
                v = kv[kt, :, half, :, :, (KV_HEADS + g) * HEAD : (KV_HEADS + g + 1) * HEAD].reshape(keys, HEAD)
                t = jnp.sum(p, axis=1, keepdims=True)
                o = jnp.dot(p.astype(BF), v, preferred_element_type=F32)
                total = t if total is None else total + t
                acc = o if acc is None else acc + o
            if first:
                tops[chunk, g] = top
                sums[chunk, g] = total
                accs[chunk, g] = acc
            else:
                fade = jnp.exp2((tops[chunk, g] - top) * SCALE)
                total = total + sums[chunk, g] * fade
                acc = acc + accs[chunk, g] * fade
                out = (acc / total).astype(BF)
                for i in range(per):
                    att[chunk, mine, :, (g * per + i) * HEAD : (g * per + i + 1) * HEAD] = out[
                        i * tok : (i + 1) * tok
                    ]

    def first_half(chunk):
        attend(chunk, me.h, True)

        @pl.when(lax.rem(chunk, 2) == 1)
        def _():
            ring_step(2 + lax.div(chunk, 2))

    loop(CH, first_half)
    w_pass(ring)

    for n in range(2):
        kv_wait(n, me.y, 1 - me.h, me.c)
        for k in (0, 2, 1):
            kv_go(n, me.y, 1 - me.h, me.c, ys[k])
        kv_go(n, me.y, 1 - me.h, me.c, sib)
    ring_step(4)
    both(1, w_pass)

    loads[6].wait()
    loads[7].wait()
    gains[me.c] = jnp.broadcast_to(gain_ref[...], (8, 256))
    theirs = pl.multiple_of((1 - me.c) * HALF, 128)
    c_copies = [
        send(gu_ref.at[:, pl.ds(theirs, HALF)], wgs.at[:, pl.ds(0, HALF)], c_s.at[0], c_r.at[0], sib),
        send(gu_ref.at[:, pl.ds(theirs + FF, HALF)], wgs.at[:, pl.ds(HALF, HALF)], c_s.at[1], c_r.at[1], sib),
        send(gains.at[me.c], gains.at[me.c], c_s.at[2], c_r.at[2], sib),
    ]
    for n in range(2):
        for k in (1, 3, 2):
            y = rem(me.y - k, NY)
            kv_wait(n, y, 1 - me.h, me.c)
            kv_go(n, y, 1 - me.h, me.c, sib)
    ring_step(5)
    both(2, w_pass)
    for n in range(2):
        for y in range(NY):
            kv_wait(n, y, 1 - me.h, 1 - me.c)
    for copy in c_copies:
        copy.start()

    def who(k):
        return rem(me.y + k, NY) * 2 + me.c

    def att_full(chunk, w, out, dev):
        part = att.at[chunk, w]
        return send(part, part, at_s.at[chunk, out], at_r.at[chunk, w], dev)

    def att_half(chunk, w, part, out, dev):
        cols = att.at[chunk, w, :, pl.ds(part * (D // 2), D // 2)]
        return send(cols, cols, at_s.at[chunk, out], ah_r.at[chunk, part], dev)

    up, down_y = ys[0], ys[2]

    def att_send(chunk, i):
        if i < 3:
            return att_full(chunk, mine, i, (up, down_y, sib)[i])
        if i < 5:
            return att_half(chunk, who((-1, 1)[i - 3]), i - 3, i, (up, down_y)[i - 3])
        return att_full(chunk, who((-1, 1, 2)[i - 5]), i, sib)

    def pass_on(chunk):
        att_full(chunk, who(-1), 0, up).wait_recv()
        att_send(chunk, 3).start()
        att_full(chunk, who(1), 0, up).wait_recv()
        for i in (4, 5, 6):
            att_send(chunk, i).start()

    def pass_last(chunk):
        att_half(chunk, who(2), 0, 0, up).wait_recv()
        att_half(chunk, who(2), 1, 0, up).wait_recv()
        att_send(chunk, 7).start()

    def second_half(chunk):
        attend(chunk, 1 - me.h, False)
        for i in range(3):
            att_send(chunk, i).start()

        @pl.when(chunk < 3)
        def _():
            ring_step(6 + chunk)

        both(chunk + 3, w_pass)

        @pl.when(chunk > 0)
        def _():
            pass_on(chunk - 1)

        @pl.when(chunk > 1)
        def _():
            pass_last(chunk - 2)

    loop(CH, second_half)
    pass_on(CH - 1)
    pass_last(CH - 2)

    def w_arrive(half):
        def one(z):
            shard = half * NZ + z
            for i in (2, 3):
                w_x_wait(shard, i)

        loop(NZ, one)

    both(NZ - 1, w_pass)
    w_pass(rem(ring - NZ, 2 * NZ))
    w_arrive(1 - me.h)

    def p_copy(chunk):
        return send(psend.at[chunk], precv.at[chunk], p_s.at[chunk], p_r.at[chunk], mate)

    def rows_of(chunk):
        return att[chunk].reshape(8 * tok, D)

    def for_mate(chunk):
        for y in range(NY):
            att_full(chunk, y * 2 + 1 - me.c, 0, sib).wait_recv()
        psend[chunk] = jnp.dot(rows_of(chunk), wb[1 - me.h].reshape(D, 256), preferred_element_type=F32).astype(BF)
        p_copy(chunk).start()

    loop(CH - 1, for_mate)
    pass_last(CH - 1)
    loop(CH, for_mate, CH - 1)
    w_arrive(me.h)
    loads[9].wait()

    def put(chunk, half, value):
        for j in range(8):
            y, c = j // 2, j % 2
            mixed[half, y, c, chunk] = res_ref[y, half, c, chunk].astype(F32) + value[j * tok : (j + 1) * tok].astype(
                F32
            )

    def for_me(chunk):
        put(chunk, me.h, jnp.dot(rows_of(chunk), wb[me.h].reshape(D, 256), preferred_element_type=F32))

    loop(CH, for_me)

    def pick(half):
        rows = (mixed[half].reshape(512, 256) * gain_ref[...]).astype(BF)
        return jnp.dot(place_t[half], rows, preferred_element_type=F32)

    picked[...] = pick(me.h)

    def from_mate(chunk):
        p_copy(chunk).wait_recv()
        put(chunk, 1 - me.h, precv[chunk])

    loop(CH, from_mate)
    disp[...] = (picked[...] + pick(1 - me.h)).astype(BF).reshape(32, 16, 256)

    def d_copy(o):
        e = peer(o)
        return send(disp.at[e], arr.at[me.exp], d_s.at[o], d_r.at[me.exp], peer_dev(e))

    loop(NX * NZ, lambda o: d_copy(o).start(), 1)
    arr[me.exp] = disp[me.exp]
    def src_x(q):
        return rem(me.x - q, NX)

    def a_copy(q):
        x = src_x(q)
        part = arr.at[pl.ds(x * NZ, NZ)]
        return send(part, sarr.at[pl.ds(x * NZ, NZ)], a_s.at[x], a_r.at[x], sib)

    def collect(q):
        x = src_x(q)

        def one(z):
            e = x * NZ + z

            @pl.when(e != me.exp)
            def _():
                send(disp.at[0], arr.at[e], d_s.at[0], d_r.at[e], sib).wait_recv()

        loop(NZ, one)
        a_copy(q).start()

    for q in range(CH):
        collect(q)
    loads[8].wait()
    c_copies[0].wait_recv()
    c_copies[1].wait_recv()
    send(gains.at[me.c], gains.at[1 - me.c], c_s.at[2], c_r.at[2], sib).wait_recv()
    ours = pl.multiple_of(me.c * HALF, 128)

    def y_copy(q, k):
        there = rem(me.y + k, NY)
        part = pb.at[q, pl.ds(there * 32, 32)]
        return send(part, yr.at[q, k - 1], y_s.at[q, k - 1], y_r.at[q, k - 1], ys[k - 1])

    def gate_up(q):
        x = src_x(q)
        a_copy(q).wait_recv()
        mine = arr[pl.ds(x * NZ, NZ)].reshape(128, 256)
        other = sarr[pl.ds(x * NZ, NZ)].reshape(128, 256)
        a = mine.astype(F32) / gains[me.c, 0:1]
        b = other.astype(F32) / gains[1 - me.c, 0:1]
        squares = jnp.sum(a * a, axis=1, keepdims=True) + jnp.sum(b * b, axis=1, keepdims=True)
        pb[q, :, FF * 1 :] = pieces(squares, 128)
        gate = jnp.dot(mine, gu_ref[:, pl.ds(ours, HALF)], preferred_element_type=F32)
        gate += jnp.dot(other, wgs[:, 0:HALF], preferred_element_type=F32)
        pb[q, :, 0:HALF] = gate.astype(BF)
        up = jnp.dot(mine, gu_ref[:, pl.ds(ours + FF, HALF)], preferred_element_type=F32)
        up += jnp.dot(other, wgs[:, HALF:FF], preferred_element_type=F32)
        pb[q, :, HALF:FF] = up.astype(BF)

    def y_send(q):
        for k in (1, 3, 2):
            y_copy(q, k).start()

    def z_copy(q):
        part = zb.at[q, pl.ds((1 - me.h) * 16, 16)]
        return send(part, zr.at[q], z_s.at[q], z_r.at[q], mate)

    def y_sum(q):
        total = pb[q, pl.ds(pl.multiple_of(me.y * 32, 32), 32)].astype(F32)
        for k in (1, 2, 3):
            y_copy(q, k).wait_recv()
            total = total + yr[q, k - 1].astype(F32)
        zb[q, :, 0:FF] = total[:, 0:FF].astype(BF)
        zb[q, :, FF:] = pieces(jnp.sum(total[:, FF:], axis=1, keepdims=True), 32)
        z_copy(q).start()


    def az_copy(q):
        part = act.at[q, me.c, me.y, me.h]
        return send(part, part, az_s.at[q], az_r.at[q], mate)

    def activate(q):
        z_copy(q).wait_recv()
        total = zb[q, pl.ds(pl.multiple_of(me.h * 16, 16), 16)].astype(F32) + zr[q].astype(F32)
        squares = jnp.sum(total[:, FF:], axis=1, keepdims=True)
        scale = lax.rsqrt(squares / D + 1e-6)
        gate = total[:, 0:HALF] * scale
        up = total[:, HALF:FF] * scale
        act[q, me.c, me.y, me.h] = (gate / (1.0 + jnp.exp(-gate)) * up).astype(BF)
        az_copy(q).start()


    def ay_copy(q, y, k):
        part = act.at[q, me.c, y]
        return send(part, part, ay_s.at[q, k - 1], ay_r.at[q, y], ys[k - 1])

    def spread(q):
        part = act.at[q, me.c, me.y, 1 - me.h]
        send(part, part, az_s.at[q], az_r.at[q], mate).wait_recv()
        for k in (1, 2, 3):
            ay_copy(q, me.y, k).start()


    def ac_copy(q, c):
        part = act.at[q, c]
        return send(part, part, ac_s.at[q], ac_r.at[q], sib)

    def share(q):
        for k in (1, 2, 3):
            ay_copy(q, rem(me.y - k, NY), k).wait_recv()
        ac_copy(q, me.c).start()


    def e_copy(o):
        e = peer(o)
        return send(eo.at[e], rb.at[me.exp], e_s.at[o], e_r.at[me.exp], peer_dev(e))

    def down(q):
        x = src_x(q)
        ac_copy(q, 1 - me.c).wait_recv()
        value = jnp.dot(act[q, 0].reshape(128, HALF), wd_ref[0:HALF], preferred_element_type=F32)
        value += jnp.dot(act[q, 1].reshape(128, HALF), wd_ref[HALF:FF], preferred_element_type=F32)
        eo[pl.ds(x * NZ, NZ)] = value.astype(BF).reshape(NZ, 16, 256)

        def back(z):
            e_copy((NX - q) % NX * NZ + z).start()

        loop(NZ, back, 1 if q == 0 else 0)

    gate_up(0)
    y_send(0)
    gate_up(1)
    y_send(1)
    gate_up(2)
    gate_up(3)
    y_sum(0)
    y_send(2)
    y_sum(1)
    y_send(3)
    y_sum(2)
    activate(0)
    y_sum(3)
    activate(1)
    activate(2)
    spread(0)
    activate(3)
    spread(1)
    share(0)
    spread(2)
    share(1)
    down(0)
    spread(3)
    share(2)
    down(1)
    share(3)
    down(2)
    down(3)
    rb[me.exp] = eo[me.exp]

    def home(e):
        @pl.when(e != me.exp)
        def _():
            send(eo.at[0], rb.at[e], e_s.at[0], e_r.at[e], sib).wait_recv()

    loop(NX * NZ, home)
    back = rb[...].reshape(slots, 256)
    for half in range(2):
        got = jnp.dot(place_ref[half], back, preferred_element_type=F32)
        value = mixed[half].reshape(512, 256) + share_ref[half] * got
        out_ref[:, half] = value.astype(BF).reshape(NY, 128, 256)

    for copy in c_copies + kv_copies:
        copy.wait_send()

    def ring_left(s):
        w_right(s).wait_send()

        @pl.when(s < NZ)
        def _():
            w_left(s).wait_send()

    loop(NZ + 1, ring_left, 1)

    def x_left(shard):
        for i in range(4):
            w_x(shard, i).wait_send()

    loop(2 * NZ, x_left)

    def peers_left(o):
        d_copy(o).wait_send()
        e_copy(o).wait_send()

    loop(NX * NZ, peers_left, 1)

    def chunk_left(q):
        for i in range(8):
            att_send(q, i).wait_send()
        p_copy(q).wait_send()
        a_copy(q).wait_send()
        z_copy(q).wait_send()
        az_copy(q).wait_send()
        ac_copy(q, me.c).wait_send()
        for k in (1, 2, 3):
            y_copy(q, k).wait_send()
            ay_copy(q, me.y, k).wait_send()

    loop(CH, chunk_left)


def body(queries, new_kv, past_kv, residual, out_weight, norm_gain, routes, gates, w_gate_up, w_down):
    sem = pltpu.SemaphoreType.DMA
    wide = FF + EXT
    out = pl.pallas_call(
        layer_kernel,
        out_shape=jax.ShapeDtypeStruct((NY, 2, 128, 256), BF),
        in_specs=[pl.BlockSpec(memory_space=pl.ANY)] * 10,
        out_specs=pl.BlockSpec(memory_space=pltpu.VMEM),
        scratch_shapes=[
            pltpu.VMEM((CH, 16, D), BF),
            pltpu.VMEM((2, NY, 2, 2, 64, 512), BF),
            pltpu.VMEM((2, 32, 128, 256), BF),
            pltpu.VMEM((NY, 2, 2, CH, 16, 256), BF),
            pltpu.VMEM((1, 256), F32),
            pltpu.VMEM((16, 8, 64), jnp.int32),
            pltpu.VMEM((16, 8, 64), F32),
            pltpu.VMEM((256, 2 * FF), BF),
            pltpu.VMEM((FF, 256), BF),
            pltpu.VMEM((CH, 8, 16, D), BF),
            pltpu.VMEM((CH, KV_HEADS, 256, HEAD), F32),
            pltpu.VMEM((CH, KV_HEADS, 256, 1), F32),
            pltpu.VMEM((CH, KV_HEADS, 256, 1), F32),
            pltpu.VMEM((256, 1024), F32),
            pltpu.VMEM((CH, 128, 256), BF),
            pltpu.VMEM((CH, 128, 256), BF),
            pltpu.VMEM((2, NY, 2, CH, 16, 256), F32),
            pltpu.VMEM((2, 512, 512), BF),
            pltpu.VMEM((2, 512, 512), BF),
            pltpu.VMEM((2, 512, 1), F32),
            pltpu.VMEM((2, 8, 256), F32),
            pltpu.VMEM((256, FF), BF),
            pltpu.VMEM((512, 256), F32),
            pltpu.VMEM((32, 16, 256), BF),
            pltpu.VMEM((32, 16, 256), BF),
            pltpu.VMEM((32, 16, 256), BF),
            pltpu.VMEM((CH, 128, wide), BF),
            pltpu.VMEM((CH, 3, 32, wide), BF),
            pltpu.VMEM((CH, 32, wide), BF),
            pltpu.VMEM((CH, 16, wide), BF),
            pltpu.VMEM((CH, 2, NY, 2, 16, HALF), BF),
            pltpu.VMEM((32, 16, 256), BF),
            pltpu.VMEM((32, 16, 256), BF),
            sem((10,)),
            sem((30,)), sem((2, NY, 2, 2)),
            sem((2, 8)), sem((16,)),
            sem((4, 16)), sem((4, 16)),
            sem((CH, 8)), sem((CH, 8)), sem((CH, 2)),
            sem((CH,)), sem((CH,)),
            sem((3,)), sem((3,)),
            sem((32,)), sem((32,)),
            sem((4,)), sem((4,)),
            sem((CH, 3)), sem((CH, 3)),
            sem((CH,)), sem((CH,)),
            sem((CH,)), sem((CH,)),
            sem((CH, 3)), sem((CH, NY)),
            sem((CH,)), sem((CH,)),
            sem((32,)), sem((32,)),
        ],
        compiler_params=pltpu.CompilerParams(
            collective_id=0, has_side_effects=True, vmem_limit_bytes=56 * 2**20
        ),
        name="layer",
    )(
        queries.reshape(CH, 16, D),
        new_kv.reshape(64, 512),
        past_kv.reshape(64, 512),
        out_weight,
        residual.reshape(NY, 2, 2, CH, 16, 256),
        norm_gain.reshape(1, 256),
        jnp.swapaxes(routes.reshape(16, 64, 8), 1, 2),
        jnp.swapaxes(gates.reshape(16, 64, 8), 1, 2),
        w_gate_up.reshape(256, 2 * FF),
        w_down.reshape(FF, 256),
    )
    return out.reshape(16, 1, 64, 256)


def solution(mesh):
    in_specs = (
        P("ctx", "exp", None, None),
        P("ctx", "exp", None, None),
        P("ctx", "exp", None, None),
        P(None, "exp", None, "ctx"),
        P("exp", "ctx"),
        P("ctx"),
        P(None, "exp", None, None),
        P(None, "exp", None, None),
        P("exp", "ctx", None),
        P("exp", None, "ctx"),
    )
    return jax.shard_map(
        body, mesh=mesh, in_specs=in_specs, out_specs=P(None, "exp", None, "ctx"), check_vma=False
    )
```

time: 211 us -> 177 us (0.84)
  Pallas kernels: 203 us -> 175 us
  local copies, waits for them, and re-layouts: 7.65 us -> 1.88 us
    pallas_call x2 -> x1, Pallas kernels: 203 us -> 175 us  [body(): pl.pallas_call(layer_kernel, out_shape=jax.ShapeDtypeStruct((NY, 2, 128,...]
    unnamed x19 -> x1, local copies, waits for them, and re-layouts: 7.65 us -> 1.88 us
where the time goes in v2:
time: 177 us
  Pallas kernels  175 us (99%)
  local copies, waits for them, and re-layouts  1.88 us (1%)
    pallas_call x1, Pallas kernels, body(): pl.pallas_call(layer_kernel, out_shape=jax.ShapeDtypeStruct((NY, 2, 128,...  175 us

profile of v2, /device:TPU:1, one launch (start us, length us, event | category | flops | bytes accessed | tf_op | source)
XLA Modules:
  0.0 176.8 jit_solution(15727571990625488266)
XLA Ops:
  0.0 174.9 %layer.1 = bf16[4,2,128,256]{3,2,1,0:T(8,128)(2,1)} custom-call(bf16[4,16,4096]{2,1,0:T(8,128)(2,1)} %bitcast.19, bf16[64,512]{1,0:T(8,128)(2,1)} %bitcast.21, bf16[64,512]{1,0:T(8,128)(2,1)} %bitcast.22, bf16[128,256]{1,0:T(8,128)(2,1)} %w_hbm.1, bf16[4,2,2,4,16,256]{5,4,3,2,1,0:T(8,128)(2,1)} %bitcast.20, f32[1,256]{1,0:T(1,128)} %bitcast.25, ...), custom_call_target="tpu_custom_call" | custom-call | tf_op jit(solution)/shard_map/layer/pallas_call | solution.py:680
  174.9 1.9 %copy.13 = bf16[16,1,64,256]{3,2,1,0:T(8,128)(2,1)} copy(bf16[16,1,64,256]{3,2,1,0:T(8,128)(2,1)} %bitcast.16) | data formatting | bytes 1048576

commit v3 on v2

--- a/solution.py
+++ b/solution.py
@@ -471,8 +471,18 @@
         e = peer(o)
         return send(disp.at[e], arr.at[me.exp], d_s.at[o], d_r.at[me.exp], peer_dev(e))
 
-    loop(NX * NZ, lambda o: d_copy(o).start(), 1)
+    def d_start(o):
+        d_copy(o).start()
+
+    def d_left(o):
+        d_copy(o).wait_send()
+
+    loop(2 * NZ, d_start, 1)
     arr[me.exp] = disp[me.exp]
+    loop(NZ, d_left, 1)
+    loop(3 * NZ, d_start, 2 * NZ)
+    loop(2 * NZ, d_left, NZ)
+    loop(4 * NZ, d_start, 3 * NZ)
     def src_x(q):
         return rem(me.x - q, NX)
 
@@ -494,8 +504,31 @@
         loop(NZ, one)
         a_copy(q).start()
 
-    for q in range(CH):
-        collect(q)
+    for copy in c_copies + kv_copies:
+        copy.wait_send()
+
+    def ring_left(s):
+        w_right(s).wait_send()
+
+        @pl.when(s < NZ)
+        def _():
+            w_left(s).wait_send()
+
+    loop(NZ + 1, ring_left, 1)
+
+    def x_left(shard):
+        for i in range(4):
+            w_x(shard, i).wait_send()
+
+    loop(2 * NZ, x_left)
+
+    def att_left(q):
+        for i in range(8):
+            att_send(q, i).wait_send()
+        p_copy(q).wait_send()
+
+    loop(CH, att_left)
+    collect(0)
     loads[8].wait()
     c_copies[0].wait_recv()
     c_copies[1].wait_recv()
@@ -593,14 +626,17 @@
 
         loop(NZ, back, 1 if q == 0 else 0)
 
+    collect(1)
     gate_up(0)
     y_send(0)
+    collect(2)
     gate_up(1)
     y_send(1)
+    collect(3)
     gate_up(2)
-    gate_up(3)
     y_sum(0)
     y_send(2)
+    gate_up(3)
     y_sum(1)
     y_send(3)
     y_sum(2)
@@ -623,46 +659,7 @@
     down(3)
     rb[me.exp] = eo[me.exp]
 
-    def home(e):
-        @pl.when(e != me.exp)
-        def _():
-            send(eo.at[0], rb.at[e], e_s.at[0], e_r.at[e], sib).wait_recv()
-
-    loop(NX * NZ, home)
-    back = rb[...].reshape(slots, 256)
-    for half in range(2):
-        got = jnp.dot(place_ref[half], back, preferred_element_type=F32)
-        value = mixed[half].reshape(512, 256) + share_ref[half] * got
-        out_ref[:, half] = value.astype(BF).reshape(NY, 128, 256)
-
-    for copy in c_copies + kv_copies:
-        copy.wait_send()
-
-    def ring_left(s):
-        w_right(s).wait_send()
-
-        @pl.when(s < NZ)
-        def _():
-            w_left(s).wait_send()
-
-    loop(NZ + 1, ring_left, 1)
-
-    def x_left(shard):
-        for i in range(4):
-            w_x(shard, i).wait_send()
-
-    loop(2 * NZ, x_left)
-
-    def peers_left(o):
-        d_copy(o).wait_send()
-        e_copy(o).wait_send()
-
-    loop(NX * NZ, peers_left, 1)
-
     def chunk_left(q):
-        for i in range(8):
-            att_send(q, i).wait_send()
-        p_copy(q).wait_send()
         a_copy(q).wait_send()
         z_copy(q).wait_send()
         az_copy(q).wait_send()
@@ -672,6 +669,24 @@
             ay_copy(q, me.y, k).wait_send()
 
     loop(CH, chunk_left)
+    loop(4 * NZ, d_left, 2 * NZ)
+
+    def home(e):
+        @pl.when(e != me.exp)
+        def _():
+            send(eo.at[0], rb.at[e], e_s.at[0], e_r.at[e], sib).wait_recv()
+
+    loop(NX * NZ, home)
+    back = rb[...].reshape(slots, 256)
+    for half in range(2):
+        got = jnp.dot(place_ref[half], back, preferred_element_type=F32)
+        value = mixed[half].reshape(512, 256) + share_ref[half] * got
+        out_ref[:, half] = value.astype(BF).reshape(NY, 128, 256)
+
+    def e_left(o):
+        e_copy(o).wait_send()
+
+    loop(NX * NZ, e_left, 1)
 
 
 def body(queries, new_kv, past_kv, residual, out_weight, norm_gain, routes, gates, w_gate_up, w_down):

time: 177 us -> 174 us (0.983); the launches traced: 177 us -> 172 us
  Pallas kernels: 175 us -> 170 us
    pallas_call x1, Pallas kernels: 175 us -> 170 us  [body(): pl.pallas_call(layer_kernel, out_shape=jax.ShapeDtypeStruct((NY, 2, 128,...]
where the time goes in v3:
time: 174 us; the launch traced here: 172 us
  Pallas kernels  170 us (98%)
  local copies, waits for them, and re-layouts  1.88 us (1%)
    pallas_call x1, Pallas kernels, body(): pl.pallas_call(layer_kernel, out_shape=jax.ShapeDtypeStruct((NY, 2, 128,...  170 us

profile of v3, /device:TPU:1, one launch (start us, length us, event | category | flops | bytes accessed | tf_op | source)
XLA Modules:
  0.0 172.0 jit_solution(771505278821670102)
XLA Ops:
  0.0 170.1 %layer.1 = bf16[4,2,128,256]{3,2,1,0:T(8,128)(2,1)} custom-call(bf16[4,16,4096]{2,1,0:T(8,128)(2,1)} %bitcast.19, bf16[64,512]{1,0:T(8,128)(2,1)} %bitcast.21, bf16[64,512]{1,0:T(8,128)(2,1)} %bitcast.22, bf16[128,256]{1,0:T(8,128)(2,1)} %w_hbm.1, bf16[4,2,2,4,16,256]{5,4,3,2,1,0:T(8,128)(2,1)} %bitcast.20, f32[1,256]{1,0:T(1,128)} %bitcast.25, ...), custom_call_target="tpu_custom_call" | custom-call | tf_op jit(solution)/shard_map/layer/pallas_call | solution.py:695
  170.1 1.9 %copy.13 = bf16[16,1,64,256]{3,2,1,0:T(8,128)(2,1)} copy(bf16[16,1,64,256]{3,2,1,0:T(8,128)(2,1)} %bitcast.16) | data formatting | bytes 1048576

commit v4 on v3

--- a/solution.py
+++ b/solution.py
@@ -409,8 +409,6 @@
             pass_last(chunk - 2)
 
     loop(CH, second_half)
-    pass_on(CH - 1)
-    pass_last(CH - 2)
 
     def w_arrive(half):
         def one(z):
@@ -436,9 +434,13 @@
         psend[chunk] = jnp.dot(rows_of(chunk), wb[1 - me.h].reshape(D, 256), preferred_element_type=F32).astype(BF)
         p_copy(chunk).start()
 
-    loop(CH - 1, for_mate)
+    for_mate(0)
+    pass_on(CH - 1)
+    for_mate(1)
+    pass_last(CH - 2)
+    for_mate(2)
     pass_last(CH - 1)
-    loop(CH, for_mate, CH - 1)
+    for_mate(3)
     w_arrive(me.h)
     loads[9].wait()
 

time: 174 us -> 170 us (0.977); the launches traced: 172 us -> 170 us
  Pallas kernels: 170 us -> 168 us
    pallas_call x1, Pallas kernels: 170 us -> 168 us  [body(): pl.pallas_call(layer_kernel, out_shape=jax.ShapeDtypeStruct((NY, 2, 128,...]
where the time goes in v4:
time: 170 us
  Pallas kernels  168 us (99%)
  local copies, waits for them, and re-layouts  1.88 us (1%)
    pallas_call x1, Pallas kernels, body(): pl.pallas_call(layer_kernel, out_shape=jax.ShapeDtypeStruct((NY, 2, 128,...  168 us

profile of v4, /device:TPU:1, one launch (start us, length us, event | category | flops | bytes accessed | tf_op | source)
XLA Modules:
  0.0 170.2 jit_solution(10775345714824246034)
XLA Ops:
  0.0 168.3 %layer.1 = bf16[4,2,128,256]{3,2,1,0:T(8,128)(2,1)} custom-call(bf16[4,16,4096]{2,1,0:T(8,128)(2,1)} %bitcast.19, bf16[64,512]{1,0:T(8,128)(2,1)} %bitcast.21, bf16[64,512]{1,0:T(8,128)(2,1)} %bitcast.22, bf16[128,256]{1,0:T(8,128)(2,1)} %w_hbm.1, bf16[4,2,2,4,16,256]{5,4,3,2,1,0:T(8,128)(2,1)} %bitcast.20, f32[1,256]{1,0:T(1,128)} %bitcast.25, ...), custom_call_target="tpu_custom_call" | custom-call | tf_op jit(solution)/shard_map/layer/pallas_call | solution.py:697
  168.3 1.9 %copy.13 = bf16[16,1,64,256]{3,2,1,0:T(8,128)(2,1)} copy(bf16[16,1,64,256]{3,2,1,0:T(8,128)(2,1)} %bitcast.16) | data formatting | bytes 1048576
